TPU v7x, 256 devices: a whole 4x4x8 slice. The times are simulated.
256 devices in a mesh: island: 16 (over y_hi, x, core), fsdp: 16 (over y_lo, z).
Axes of the slice: x: 4, y: 4 (y_hi: 2, y_lo: 2; y = y_hi * 2 + y_lo), z: 8, core: 2. Of those that a mesh axis runs over, the one named last changes fastest.
Arguments:
- normed: bfloat16 [2, 49152, 8192], P(None, ('island', 'fsdp')), may hold values from -6 to 6
- value_weight: bfloat16 [16, 8192, 512], P('island', 'fsdp'), may hold values from -0.0625 to 0.0625
- value_cotangent: bfloat16 [2, 49152, 512], P(None, ('island', 'fsdp')), may hold values from -0.079589844 to 0.079589844
- local_fragment: bfloat16 [16, 8192, 512], P('island', 'fsdp'), may hold values from -6 to 6
- global_fragment: float32 [8192, 512], P('fsdp'), may hold values from -6 to 6
- outer_momentum: float32 [8192, 512], P('fsdp', 'island'), may hold values from -3 to 3
Outputs:
- projected: bfloat16 [2, 49152, 512], P(None, ('island', 'fsdp'))
- value_grad: float32 [16, 8192, 512], P('island', 'fsdp')
- new_global: float32 [8192, 512], P('fsdp')
- new_momentum: float32 [8192, 512], P('fsdp', 'island')
All inputs are finite; a program needn't handle non-finite values.
Results may differ from a plain program's by a relative error of at most 0.001.
Values may be sent and summed in bfloat16 or wider, within the bound.
No kernel may reach another device: no remote copies, remote signals or barrier semaphores. Data moves between devices by JAX's collectives and lax.ppermute only.
A program may use at most 128 MiB of HBM per device.

v0:
```python
import jax
import jax.numpy as jnp
from jax import lax
from jax.sharding import PartitionSpec as P

outer_rate = 0.7
outer_mu = 0.9


def per_device(
    normed, value_weight, value_cotangent, local_fragment, global_fragment, outer_momentum
):
    micro_count, tok_rows, model_width = normed.shape
    kv_width = value_cotangent.shape[2]
    flat_rows = normed.reshape(micro_count * tok_rows, model_width)
    flat_cots = value_cotangent.reshape(micro_count * tok_rows, kv_width)
    columns = flat_rows
    forward = jnp.dot(
        columns,
        lax.all_gather(value_weight[0], "fsdp", axis=0, tiled=True),
        preferred_element_type=jnp.float32,
    )
    projected = forward.astype(jnp.bfloat16).reshape(micro_count, tok_rows, kv_width)
    columns = flat_rows
    gradient = lax.psum_scatter(
        lax.dot_general(
            columns, flat_cots, (((0,), (0,)), ((), ())), preferred_element_type=jnp.float32
        ),
        "fsdp",
        scatter_dimension=0,
        tiled=True,
    )
    value_grad = gradient[None]
    islands = lax.axis_size("island")
    own_delta = global_fragment - local_fragment[0].astype(jnp.float32)
    col_width = outer_momentum.shape[1]
    position = lax.axis_index("island")
    pseudo = lax.psum(own_delta, "island") / islands
    shared = lax.dynamic_slice_in_dim(pseudo, position * col_width, col_width, 1)
    new_momentum = outer_mu * outer_momentum + shared
    full_momentum = lax.all_gather(new_momentum, "island", axis=1, tiled=True)
    new_global = global_fragment - outer_rate * (pseudo + outer_mu * full_momentum)
    return (projected, value_grad, new_global, new_momentum)


def solution(mesh):
    placed = (
        P(None, ("island", "fsdp"), None),
        P("island", "fsdp", None),
        P(None, ("island", "fsdp"), None),
        P("island", "fsdp", None),
        P("fsdp", None),
        P("fsdp", "island"),
    )
    return jax.shard_map(
        per_device,
        mesh=mesh,
        in_specs=placed,
        out_specs=(
            P(None, ("island", "fsdp"), None),
            P("island", "fsdp", None),
            P("fsdp", None),
            P("fsdp", "island"),
        ),
        check_vma=False,
    )
```

profile of v0, /device:TPU:1, one launch (start us, length us, event | category | flops | bytes accessed | tf_op | source)
XLA Modules:
  0.0 510.5 jit_solution(15630123859144068690)
XLA Ops:
  7.2 0.0 copy-start
  7.2 0.0 copy-start.2
  7.2 0.0 all-reduce.2.cloned.1.call-start
  7.2 1.6 copy.12
  8.8 1.3 copy.10
  10.1 1.1 convert_subtract_fusion
  11.2 0.0 all-reduce.2.cloned.1.call-update
  11.3 0.0 all-gather.4.cloned.1.call-start
  11.3 149.2 %all-reduce.2.cloned.1.call-done = f32[512,512]{0,1:T(8,128)} async-done(((f32[512,512]{0,1:T(8,128)}), f32[512,512]{0,1:T(8,128)}) %all-reduce.2.cloned.1.call-update) | async-done | bytes 1048592 | tf_op jit(solution)/shard_map/psum | solution.py:38
  160.5 1.3 broadcast_multiply_fusion
  161.8 0.0 copy-done.2
  161.8 0.6 dynamic-slice_add_fusion
  162.5 0.0 all-gather.4.cloned.1.call-update
  162.5 0.0 all-gather.6.cloned.1.call-start
  162.6 0.7 all-gather.6.cloned.1.call-update
  163.2 0.0 reduce-scatter.2.cloned.1.call-start
  163.3 0.0 copy-done
  163.3 11.1 %convolution_bitcast_fusion = f32[8192,512]{1,0:T(8,128)} fusion(bf16[2,192,8192]{2,1,0:T(8,128)(2,1)} %param.6, bf16[2,192,512]{2,1,0:T(8,128)(2,1)S(1)} %copy-done), kind=kOutput, calls=%fused_computation | convolution fusion | flops 3221225472 | bytes 23461888 | tf_op jit(solution)/shard_map/dot_general | solution.py:26
  174.4 0.0 copy-start.1
  174.4 0.0 reduce-scatter.2.cloned.1.call-update
  174.4 41.6 %all-gather.4.cloned.1.call-done = f32[512,512]{0,1:T(8,128)} async-done(((f32[512,32]{0,1:T(8,128)}), f32[512,512]{0,1:T(8,128)}) %all-gather.4.cloned.1.call-update) | async-done | bytes 1048592 | tf_op jit(solution)/shard_map/all_gather | solution.py:41
  216.0 0.0 copy-done.1
  216.0 1.6 multiply_subtract_fusion
  217.6 1.3 copy.13
  218.9 98.5 %all-gather.6.cloned.1.call-done = bf16[1,8192,512]{2,1,0:T(8,128)(2,1)} async-done(((bf16[1,512,512]{2,1,0:T(8,128)(2,1)}), bf16[1,8192,512]{2,1,0:T(8,128)(2,1)}) %all-gather.6.cloned.1.call-update) | async-done | bytes 8388624 | tf_op jit(solution)/shard_map/all_gather | solution.py:20
  317.4 9.3 %fusion.2 = bf16[384,512]{1,0:T(8,128)(2,1)} fusion(bf16[384,8192]{1,0:T(8,128)(2,1)} %bitcast.16, bf16[1,8192,512]{2,1,0:T(8,128)(2,1)} %all-gather.6.cloned.1.call-done), kind=kOutput, calls=%fused_computation.3 | convolution fusion | flops 3221422080 | bytes 15073280 | tf_op jit(solution)/shard_map/dot_general | solution.py:18
  326.7 177.3 %reduce-scatter.2.cloned.1.call-done = f32[512,512]{1,0:T(8,128)} async-done(((f32[8192,512]{1,0:T(8,128)}), f32[512,512]{1,0:T(8,128)}) %reduce-scatter.2.cloned.1.call-update) | async-done | bytes 1048592 | tf_op jit(solution)/shard_map/reduce_scatter | solution.py:25
Async XLA Ops:
  7.2 156.1 %copy-start = (bf16[2,192,512]{2,1,0:T(8,128)(2,1)S(1)}, bf16[2,192,512]{2,1,0:T(8,128)(2,1)}, u32[]{:S(2)}) copy-start(bf16[2,192,512]{2,1,0:T(8,128)(2,1)} %param.8) | copy-start | bytes 1179652
  7.2 154.7 %copy-start.2 = (f32[512,32]{0,1:T(8,128)S(1)}, f32[512,32]{0,1:T(8,128)}, u32[]{:S(2)}) copy-start(f32[512,32]{0,1:T(8,128)} %param.11) | copy-start | bytes 196612
  7.2 153.3 %all-reduce.2.cloned.1.call-start = ((), (), s32[]{:S(2)}) async-start(), calls=%async_computation.2 | async-start | bytes 2097152 | tf_op jit(solution)/shard_map/psum | solution.py:38
  11.3 204.7 %all-gather.4.cloned.1.call-start = ((), (), s32[]{:S(2)}) async-start(), calls=%async_computation.3 | async-start | bytes 1114112 | tf_op jit(solution)/shard_map/all_gather | solution.py:41
  162.5 154.9 %all-gather.6.cloned.1.call-start = ((), (), s32[]{:S(2)}) async-start(), calls=%async_computation.4 | async-start | bytes 8912896 | tf_op jit(solution)/shard_map/all_gather | solution.py:20
  163.2 340.7 %reduce-scatter.2.cloned.1.call-start = ((), (), s32[]{:S(2)}) async-start(), calls=%async_computation.1 | async-start | bytes 17825792 | tf_op jit(solution)/shard_map/reduce_scatter | solution.py:25
  174.4 41.6 %copy-start.1 = (f32[512,512]{0,1:T(8,128)S(1)}, f32[512,512]{0,1:T(8,128)}, u32[]{:S(2)}) copy-start(f32[512,512]{0,1:T(8,128)} %all-reduce.2.cloned.1.call-done) | copy-start | bytes 3145732
Sparse Core Ops, SparseCore 0:
  11.4 149.0 all-reduce.1
  164.2 51.7 all-gather.3
  217.9 99.4 all-gather.5
  320.5 183.4 reduce-scatter.1
where the time goes:
time: 511 us
  waiting for transfers between devices  467 us (91%)
  matrix products  20.4 us (4%)
  between operations  13.8 us (3%)
    reduce_scatter x1, waiting for transfers between devices, per_device(): lax.psum_scatter(lax.dot_general(columns, flat_cots, (((0,), (0,)), ((),...  177 us
    psum x1, waiting for transfers between devices, per_device(): pseudo = lax.psum(own_delta, 'island') / islands  149 us
    all_gather x1, waiting for transfers between devices, per_device(): lax.all_gather(value_weight[0], 'fsdp', axis=0, tiled=True)  98.5 us
    all_gather x1, waiting for transfers between devices, per_device(): full_momentum = lax.all_gather(new_momentum, 'island', axis=1, tiled=True)  41.6 us
    dot_general x1, matrix products, per_device(): lax.dot_general(columns, flat_cots, (((0,), (0,)), ((), ())), preferred_e...  11.1 us
  transfers between devices with their start and end apart: 4, of which 4 were waited for; matrix products, arithmetic and copies ran while one was open for 5% of the time, Pallas kernels for 0%

commit v1 on v0

--- a/solution.py
+++ b/solution.py
@@ -38,7 +38,9 @@
     pseudo = lax.psum(own_delta, "island") / islands
     shared = lax.dynamic_slice_in_dim(pseudo, position * col_width, col_width, 1)
     new_momentum = outer_mu * outer_momentum + shared
-    full_momentum = lax.all_gather(new_momentum, "island", axis=1, tiled=True)
+    full_momentum = jnp.concatenate(
+        lax.all_to_all(jnp.stack([new_momentum] * lax.axis_size("island")), "island", 0, 0), axis=1
+    )
     new_global = global_fragment - outer_rate * (pseudo + outer_mu * full_momentum)
     return (projected, value_grad, new_global, new_momentum)
 

time: 511 us -> 342 us (0.67)
  waiting for transfers between devices: 467 us -> 143 us
  blocking collectives: 0 us -> 155 us
    reduce_scatter x1, waiting for transfers between devices: 177 us -> 0.01 us  [per_device(): lax.psum_scatter(lax.dot_general(columns, flat_cots, (((0,), (0,)), ((),...]
    all_to_all x0 -> x1, blocking collectives: none -> 155 us  [per_device(): lax.all_to_all(jnp.stack([new_momentum] * lax.axis_size('island')), 'isla...]
    all_gather x1, waiting for transfers between devices: 98.5 us -> 0.01 us  [per_device(): lax.all_gather(value_weight[0], 'fsdp', axis=0, tiled=True)]
    all_gather x1 -> x0, waiting for transfers between devices: 41.6 us -> none  [per_device(): full_momentum = lax.all_gather(new_momentum, 'island', axis=1, tiled=True)]
    psum x1, waiting for transfers between devices: 149 us -> 143 us  [per_device(): pseudo = lax.psum(own_delta, 'island') / islands]
  transfers between devices with their start and end apart: 4 -> 3, of which waited for: 4 -> 1; matrix products, arithmetic and copies ran while one was open for 5% -> 7% of each run, Pallas kernels for 0% -> 0%
where the time goes in v1:
time: 342 us
  blocking collectives  155 us (45%)
  waiting for transfers between devices  143 us (42%)
  matrix products  20.4 us (6%)
  between operations  15.6 us (5%)
  local copies, waits for them, and re-layouts  4.3 us (1%)
    all_to_all x1, blocking collectives, per_device(): lax.all_to_all(jnp.stack([new_momentum] * lax.axis_size('island')), 'isla...  155 us
    psum x1, waiting for transfers between devices, per_device(): pseudo = lax.psum(own_delta, 'island') / islands  143 us
    dot_general x1, matrix products, per_device(): lax.dot_general(columns, flat_cots, (((0,), (0,)), ((), ())), preferred_e...  11.1 us
    dot_general x1, matrix products, per_device(): jnp.dot(columns, lax.all_gather(value_weight[0], 'fsdp', axis=0, tiled=Tr...  9.35 us
  transfers between devices with their start and end apart: 3, of which 1 were waited for; matrix products, arithmetic and copies ran while one was open for 7% of the time, Pallas kernels for 0%

profile of v1, /device:TPU:1, one launch (start us, length us, event | category | flops | bytes accessed | tf_op | source)
XLA Modules:
  0.0 342.2 jit_solution(3667573410706770057)
XLA Ops:
  8.0 0.0 copy-start
  8.0 0.0 all-reduce.2.cloned.1.call-start
  8.1 1.6 copy.12
  9.7 1.3 copy.10
  10.9 1.1 convert_subtract_fusion
  12.1 0.0 all-reduce.2.cloned.1.call-update
  12.1 0.0 all-gather.3.cloned.1.call-start
  12.1 0.5 all-gather.3.cloned.1.call-update
  12.7 0.0 reduce-scatter.2.cloned.1.call-start
  12.7 0.0 copy-done
  12.7 11.1 %convolution_bitcast_fusion = f32[8192,512]{1,0:T(8,128)} fusion(bf16[2,192,8192]{2,1,0:T(8,128)(2,1)} %param.6, bf16[2,192,512]{2,1,0:T(8,128)(2,1)S(1)} %copy-done), kind=kOutput, calls=%fused_computation | convolution fusion | flops 3221225472 | bytes 23461888 | tf_op jit(solution)/shard_map/dot_general | solution.py:26
  23.8 0.0 copy-start.3
  23.8 0.0 reduce-scatter.2.cloned.1.call-update
  23.8 142.8 %all-reduce.2.cloned.1.call-done = f32[512,512]{0,1:T(8,128)} async-done(((f32[512,512]{0,1:T(8,128)}), f32[512,512]{0,1:T(8,128)}) %all-reduce.2.cloned.1.call-update) | async-done | bytes 1048592 | tf_op jit(solution)/shard_map/psum | solution.py:38
  166.6 0.0 copy-start.1
  166.6 1.4 broadcast_multiply_fusion.1
  168.0 0.0 copy-done.3
  168.1 0.0 copy-start.2
  168.1 0.1 stack.2
  168.2 155.4 %all_to_all.5 = f32[16,512,32]{1,2,0:T(8,128)S(1)} all-to-all(f32[16,512,32]{1,2,0:T(8,128)S(1)} %stack.2), channel_id=1, replica_groups=mesh['island'=16,'fsdp'=16] {'island'}, dimensions={0} | all-to-all | bytes 2097152 | tf_op jit(solution)/shard_map/all_to_all | solution.py:42
  323.6 0.1 broadcast_multiply_fusion
  323.7 0.0 copy-done.1
  323.7 0.4 fusion.6
  324.1 1.3 copy.13
  325.4 0.0 all-gather.3.cloned.1.call-done
  325.4 9.3 %fusion.2 = bf16[384,512]{1,0:T(8,128)(2,1)} fusion(bf16[384,8192]{1,0:T(8,128)(2,1)} %bitcast.24, bf16[1,8192,512]{2,1,0:T(8,128)(2,1)} %all-gather.3.cloned.1.call-done), kind=kOutput, calls=%fused_computation.3 | convolution fusion | flops 3221422080 | bytes 15073280 | tf_op jit(solution)/shard_map/dot_general | solution.py:18
  334.8 0.0 copy-done.2
  334.8 0.0 reduce-scatter.2.cloned.1.call-done
  (1 shorter events, 0.0 us)
Async XLA Ops:
  8.0 4.7 %copy-start = (bf16[2,192,512]{2,1,0:T(8,128)(2,1)S(1)}, bf16[2,192,512]{2,1,0:T(8,128)(2,1)}, u32[]{:S(2)}) copy-start(bf16[2,192,512]{2,1,0:T(8,128)(2,1)} %param.8) | copy-start | bytes 1179652
  8.0 158.6 %all-reduce.2.cloned.1.call-start = ((), (), s32[]{:S(2)}) async-start(), calls=%async_computation.3 | async-start | bytes 2097152 | tf_op jit(solution)/shard_map/psum | solution.py:38
  12.1 313.3 %all-gather.3.cloned.1.call-start = ((), (), s32[]{:S(2)}) async-start(), calls=%async_computation.4 | async-start | bytes 8912896 | tf_op jit(solution)/shard_map/all_gather | solution.py:20
  12.7 322.1 %reduce-scatter.2.cloned.1.call-start = ((), (), s32[]{:S(2)}) async-start(), calls=%async_computation.2 | async-start | bytes 17825792 | tf_op jit(solution)/shard_map/reduce_scatter | solution.py:25
  23.8 144.2 %copy-start.3 = (f32[512,32]{0,1:T(8,128)S(1)}, f32[512,32]{0,1:T(8,128)}, u32[]{:S(2)}) copy-start(f32[512,32]{0,1:T(8,128)} %param.11) | copy-start | bytes 196612
  166.6 157.1 %copy-start.1 = (f32[512,512]{0,1:T(8,128)S(1)}, f32[512,512]{0,1:T(8,128)}, u32[]{:S(2)}) copy-start(f32[512,512]{0,1:T(8,128)} %all-reduce.2.cloned.1.call-done) | copy-start | bytes 3145732
  168.1 166.7 %copy-start.2 = (f32[512,32]{0,1:T(8,128)}, f32[512,32]{0,1:T(8,128)S(1)}, u32[]{:S(2)}) copy-start(f32[512,32]{0,1:T(8,128)S(1)} %dynamic-slice_add_fusion) | copy-start | bytes 196612
Sparse Core Ops, SparseCore 0:
  12.2 154.3 all-reduce.1
Sparse Core Ops, SparseCore 1:
  14.3 110.8 all-gather.2
  128.2 192.2 reduce-scatter.1

commit v2 on v0

--- a/solution.py
+++ b/solution.py
@@ -35,7 +35,7 @@
     own_delta = global_fragment - local_fragment[0].astype(jnp.float32)
     col_width = outer_momentum.shape[1]
     position = lax.axis_index("island")
-    pseudo = lax.psum(own_delta, "island") / islands
+    pseudo = jnp.sum(lax.all_gather(own_delta, "island"), axis=0) / islands
     shared = lax.dynamic_slice_in_dim(pseudo, position * col_width, col_width, 1)
     new_momentum = outer_mu * outer_momentum + shared
     full_momentum = lax.all_gather(new_momentum, "island", axis=1, tiled=True)

time: 511 us -> 477 us (0.933)
  waiting for transfers between devices: 467 us -> 426 us
  other arithmetic: 4.69 us -> 12 us
    psum x1 -> x0, waiting for transfers between devices: 149 us -> none  [per_device(): pseudo = lax.psum(own_delta, 'island') / islands]
    all_gather x0 -> x1, waiting for transfers between devices: none -> 119 us  [per_device(): pseudo = jnp.sum(lax.all_gather(own_delta, 'island'), axis=0) / islands]
    all_gather x1, waiting for transfers between devices: 98.5 us -> 79.8 us  [per_device(): lax.all_gather(value_weight[0], 'fsdp', axis=0, tiled=True)]
    reduce_sum x0 -> x1, other arithmetic: none -> 7.91 us  [per_device(): pseudo = jnp.sum(lax.all_gather(own_delta, 'island'), axis=0) / islands]
    reduce_scatter x1, waiting for transfers between devices: 177 us -> 184 us  [per_device(): lax.psum_scatter(lax.dot_general(columns, flat_cots, (((0,), (0,)), ((),...]
  transfers between devices with their start and end apart: 4 -> 4, of which waited for: 4 -> 4; matrix products, arithmetic and copies ran while one was open for 5% -> 7% of each run, Pallas kernels for 0% -> 0%
where the time goes in v2:
time: 477 us; the launch traced here: 476 us
  waiting for transfers between devices  426 us (89%)
  matrix products  20.8 us (4%)
  between operations  13.8 us (3%)
  other arithmetic  12 us (3%)
    reduce_scatter x1, waiting for transfers between devices, per_device(): lax.psum_scatter(lax.dot_general(columns, flat_cots, (((0,), (0,)), ((),...  184 us
    all_gather x1, waiting for transfers between devices, per_device(): pseudo = jnp.sum(lax.all_gather(own_delta, 'island'), axis=0) / islands  119 us
    all_gather x1, waiting for transfers between devices, per_device(): lax.all_gather(value_weight[0], 'fsdp', axis=0, tiled=True)  79.8 us
    all_gather x1, waiting for transfers between devices, per_device(): full_momentum = lax.all_gather(new_momentum, 'island', axis=1, tiled=True)  42.1 us
    dot_general x1, matrix products, per_device(): lax.dot_general(columns, flat_cots, (((0,), (0,)), ((), ())), preferred_e...  11.4 us
  transfers between devices with their start and end apart: 4, of which 4 were waited for; matrix products, arithmetic and copies ran while one was open for 7% of the time, Pallas kernels for 0%

profile of v2, /device:TPU:1, one launch (start us, length us, event | category | flops | bytes accessed | tf_op | source)
XLA Modules:
  0.0 476.4 jit_solution(10941836951331127705)
XLA Ops:
  7.2 0.0 copy-start
  7.2 0.0 all-gather.10.cloned.1.call-start
  7.2 2.5 convert_subtract_fusion
  9.8 0.0 all-gather.10.cloned.1.call-update
  9.8 0.0 all-gather.8.cloned.1.call-start
  9.8 0.7 all-gather.8.cloned.1.call-update
  10.5 0.0 all-gather.6.cloned.1.call-start
  10.6 1.0 copy.14
  11.6 119.4 %all-gather.10.cloned.1.call-done = f32[8192,512]{1,0:T(8,128)} async-done(((f32[512,512]{1,0:T(8,128)}), f32[8192,512]{1,0:T(8,128)}) %all-gather.10.cloned.1.call-update) | async-done | bytes 16777232 | tf_op jit(solution)/shard_map/all_gather | solution.py:38
  130.9 7.9 %reduce_sum.9 = f32[512,512]{1,0:T(8,128)S(1)} reduce(f32[16,512,512]{2,1,0:T(8,128)} %bitcast.17, f32[]{:T(128)} %constant.3.clone.1), dimensions={0}, to_apply=%region_1.0 | reduce | flops 3932160 | bytes 17825796 | tf_op jit(solution)/shard_map/reduce_sum | solution.py:38
  138.9 0.1 broadcast_multiply_fusion
  139.0 0.1 dynamic-slice_add_fusion
  139.1 0.7 copy.15
  139.8 0.0 all-gather.6.cloned.1.call-update
  139.9 0.0 reduce-scatter.2.cloned.1.call-start
  139.9 0.0 copy-done
  139.9 11.4 %convolution_bitcast_fusion = f32[8192,512]{1,0:T(8,128)} fusion(bf16[2,192,8192]{2,1,0:T(8,128)(2,1)} %param.6, bf16[2,192,512]{2,1,0:T(8,128)(2,1)S(1)} %copy-done), kind=kOutput, calls=%fused_computation | convolution fusion | flops 3221225472 | bytes 23461888 | tf_op jit(solution)/shard_map/dot_general | solution.py:26
  151.3 0.0 reduce-scatter.2.cloned.1.call-update
  151.3 79.8 %all-gather.8.cloned.1.call-done = bf16[1,8192,512]{2,1,0:T(8,128)(2,1)} async-done(((bf16[1,512,512]{2,1,0:T(8,128)(2,1)}), bf16[1,8192,512]{2,1,0:T(8,128)(2,1)}) %all-gather.8.cloned.1.call-update) | async-done | bytes 8388624 | tf_op jit(solution)/shard_map/all_gather | solution.py:20
  231.1 0.0 copy-start.1
  231.2 9.4 %fusion.2 = bf16[384,512]{1,0:T(8,128)(2,1)} fusion(bf16[384,8192]{1,0:T(8,128)(2,1)} %bitcast.18, bf16[1,8192,512]{2,1,0:T(8,128)(2,1)} %all-gather.8.cloned.1.call-done), kind=kOutput, calls=%fused_computation.3 | convolution fusion | flops 3221422080 | bytes 15073280 | tf_op jit(solution)/shard_map/dot_general | solution.py:18
  240.6 42.1 %all-gather.6.cloned.1.call-done = f32[512,512]{0,1:T(8,128)} async-done(((f32[512,32]{0,1:T(8,128)}), f32[512,512]{0,1:T(8,128)}) %all-gather.6.cloned.1.call-update) | async-done | bytes 1048592 | tf_op jit(solution)/shard_map/all_gather | solution.py:41
  282.7 1.6 copy.16
  284.3 0.0 copy-done.1
  284.3 1.3 multiply_subtract_fusion
  285.6 184.3 %reduce-scatter.2.cloned.1.call-done = f32[512,512]{1,0:T(8,128)} async-done(((f32[8192,512]{1,0:T(8,128)}), f32[512,512]{1,0:T(8,128)}) %reduce-scatter.2.cloned.1.call-update) | async-done | bytes 1048592 | tf_op jit(solution)/shard_map/reduce_scatter | solution.py:25
Async XLA Ops:
  7.2 132.8 %copy-start = (bf16[2,192,512]{2,1,0:T(8,128)(2,1)S(1)}, bf16[2,192,512]{2,1,0:T(8,128)(2,1)}, u32[]{:S(2)}) copy-start(bf16[2,192,512]{2,1,0:T(8,128)(2,1)} %param.8) | copy-start | bytes 1179652
  7.2 123.8 %all-gather.10.cloned.1.call-start = ((), (), s32[]{:S(2)}) async-start(), calls=%async_computation.4 | async-start | bytes 17825792 | tf_op jit(solution)/shard_map/all_gather | solution.py:38
  9.8 221.4 %all-gather.8.cloned.1.call-start = ((), (), s32[]{:S(2)}) async-start(), calls=%async_computation.3 | async-start | bytes 8912896 | tf_op jit(solution)/shard_map/all_gather | solution.py:20
  10.5 272.2 %all-gather.6.cloned.1.call-start = ((), (), s32[]{:S(2)}) async-start(), calls=%async_computation.2 | async-start | bytes 1114112 | tf_op jit(solution)/shard_map/all_gather | solution.py:41
  139.9 330.0 %reduce-scatter.2.cloned.1.call-start = ((), (), s32[]{:S(2)}) async-start(), calls=%async_computation.1 | async-start | bytes 17825792 | tf_op jit(solution)/shard_map/reduce_scatter | solution.py:25
  231.1 53.1 %copy-start.1 = (f32[512,512]{1,0:T(8,128)S(1)}, f32[512,512]{1,0:T(8,128)}, u32[]{:S(2)}) copy-start(f32[512,512]{1,0:T(8,128)} %param.10) | copy-start | bytes 3145732
Sparse Core Ops, SparseCore 0:
  11.3 119.5 all-gather.9
  132.7 98.3 all-gather.7
  234.5 48.2 all-gather.5
  285.7 184.1 reduce-scatter.1
